TPU v7x, 256 devices: a whole 4x4x8 slice. The times are simulated.
256 devices in a mesh: dp: 8 (over y, x_hi), tm: 32 (over z, x_lo, core).
Axes of the slice: x: 4 (x_hi: 2, x_lo: 2; x = x_hi * 2 + x_lo), y: 4, z: 8, core: 2. Of those that a mesh axis runs over, the one named last changes fastest.
Arguments:
- features: bfloat16 [8, 4096, 1024], P('dp', 'tm'), may hold values from -20 to 20
- context: bfloat16 [8, 4096, 1024], P('dp', 'tm'), may hold values from -20 to 20
- predictor: bfloat16 [1024, 2, 1024], replicated, may hold values from -0.1875 to 0.1875
- projection: bfloat16 [1024, 1024], replicated, may hold values from -0.1875 to 0.1875
- lengths: int32 [8, 32], P('dp', 'tm'), may hold values from 128 to 128, as said below
- frame_mask: int32 [8, 4096], P('dp', 'tm'), may hold values 0 or 1
Outputs:
- loss: float32 [], replicated
- grad_pred: float32 [1024, 2, 1024], P(('dp', 'tm'))
- grad_proj: float32 [1024, 1024], P(('dp', 'tm'))
Inputs may be any that keep to these rules, and one draw needn't show every extreme that they name: `lengths`: every entry is a multiple of 128; some entry equals 128.
All inputs are finite; a program needn't handle non-finite values. No bound on the sum of `frame_mask` on one device may be relied on, other than what follows from the above.
Results may differ from a plain program's by a relative error of at most 0.014.
The roundings to bfloat16 on the way count: a program that leaves them out, or rounds other values in their place, can miss the bound.
Values may be sent and summed in bfloat16 or wider, within the bound.
No kernel may reach another device: no remote copies, remote signals or barrier semaphores. Data moves between devices by JAX's collectives and lax.ppermute only.
A program may use at most 128 MiB of HBM per device.

v0:
```python
import functools

import jax
import jax.numpy as jnp
from jax import lax
from jax.experimental import pallas as pl
from jax.experimental.pallas import tpu as pltpu
from jax.sharding import Mesh, PartitionSpec as P

DP = ("y", "xh")
TM = ("z", "xl", "core")
ALL = DP + TM
PLANE = ("xh", "z", "xl")
RING = ("y", "core")
CHIPS = ("y", "xh", "z", "xl")
F32 = jnp.float32
BF16 = jnp.bfloat16
REACH = 2


def size_of(names):
    size = 1
    for name in names:
        size *= lax.axis_size(name)
    return size


def ring_shift(block, axes, offset):
    size = size_of(axes)
    return lax.ppermute(block, axes, [((i + offset) % size, i) for i in range(size)])


def window_at(block, offset):
    return ring_shift(block, TM, offset)


def other_core(block):
    return lax.ppermute(block, "core", [(0, 1), (1, 0)])


def rows_dot(a, b):
    return lax.dot_general(a, b, (((1,), (1,)), ((), ())), preferred_element_type=F32)


def cols_dot(a, b):
    return lax.dot_general(a, b, (((0,), (0,)), ((), ())), preferred_element_type=F32)


def flag_terms(horizons, windows, device, tm, flags):
    chips, span = flags.shape
    frames = span // 2
    row = lax.broadcasted_iota(jnp.int32, flags.shape, 0)
    lane = lax.broadcasted_iota(jnp.int32, flags.shape, 1)
    last = row % (windows // 2) == windows // 2 - 1
    following = jnp.where(last, 0.0, pltpu.roll(flags, chips - 1, 0))
    slot = lax.broadcasted_iota(jnp.int32, (chips, 16), 1)
    source = lax.broadcasted_iota(jnp.int32, (chips, 16), 0)

    def picked(values, reach, transposed):
        window = slot - reach
        inside = (tm + window >= 0) & (tm + window < windows)
        out = 0.0
        for half in range(2):
            pick = (2 * source + half == device + window) & inside
            pick = jnp.where(pick, 1.0, 0.0).astype(BF16)
            part = values[:, half * frames : (half + 1) * frames].astype(BF16)
            out = out + (cols_dot(part, pick) if transposed else cols_dot(pick, part))
        return out

    total = jnp.zeros((1, span), F32)
    act = []
    for h in range(1, horizons + 1):
        ahead = jnp.where(
            lane < span - h, pltpu.roll(flags, span - h, 1), pltpu.roll(following, span - h, 1)
        )
        pairs = flags * ahead
        total = total + jnp.sum(pairs, axis=0, keepdims=True)
        act.append(picked(pairs, REACH, True))
    count = jnp.sum(total, axis=1, keepdims=True)
    return count, picked(flags, 2 * REACH, False), jnp.concatenate(act, axis=0)


def stacked_dot(rows, weights, out_ref):
    windows, stacked, width = out_ref.shape
    tile = 512
    frames = stacked * width // weights.shape[1]
    for at in range(0, weights.shape[1], tile):
        part = jnp.dot(rows, weights[:, at : at + tile], preferred_element_type=F32).astype(BF16)
        step, lane = divmod(at, width)
        for w in range(windows):
            out_ref[w, step * frames : (step + 1) * frames, lane : lane + tile] = part[
                w * frames : (w + 1) * frames
            ]


def pred_kernel(low2, ctx, high2, weights, out_ref, done_ref, rows, sems):
    frames = ctx.shape[0]
    copies = [
        pltpu.make_async_copy(block, rows.at[pl.ds(slot * frames, frames)], sems.at[slot])
        for slot, block in enumerate(
            (low2.at[pl.ds(frames, frames)], ctx, high2.at[pl.ds(frames, frames)])
        )
    ]
    for copy in copies:
        copy.start()
    for copy in copies:
        copy.wait()
    stacked_dot(rows[...], weights, out_ref)
    done_ref[...] = jnp.zeros_like(done_ref)


def delta_kernel(
    horizons, windows, core_ref, flags_ref, preds_ref, weights,
    both, low2, high2, low4, high4, both_x, low2_x, high2_x, low4_x, high4_x,
    out_0, out_1, out_2, out_3, loss_ref, codes, code_acc, odd_ctx, odd_pred, blocks, sems,
):
    frames, width = low4.shape
    scale = width ** (-0.5)
    ring, cores = blocks.shape[:2]
    parts = ring * cores
    pred_cols, code_cols = horizons * width // parts, width // parts
    core, place = core_ref[0, 0], core_ref[0, 1]

    def put(sem, block, start, held, slot):
        at = slot * frames
        if not isinstance(slot, int):
            at = pl.multiple_of(at, frames)
        return pltpu.make_async_copy(
            block.at[pl.ds(start, frames)], held.at[pl.ds(at, frames)], sems.at[sem]
        )

    ctx_copies = [
        put(0, low2_x, frames, odd_ctx, 1 - core),
        put(1, both_x, frames, odd_ctx, 2 - core),
        put(2, high2_x, frames, odd_ctx, 3 - core),
    ]
    code_copies = [
        put(3, low4, 0, codes, 1),
        put(4, low2, 0, codes, 3),
        put(5, both, 0, codes, 5),
        put(6, high2, 0, codes, 7),
        put(7, high4, 0, codes, 9),
        put(8, low4_x, 0, codes, 2 - 2 * core),
        put(9, low2_x, 0, codes, 4 - 2 * core),
        put(10, both_x, 0, codes, 6 - 2 * core),
        put(11, high2_x, 0, codes, 8 - 2 * core),
        put(12, high4_x, 0, codes, 10 - 2 * core),
    ]
    for copy in ctx_copies + code_copies:
        copy.start()
    for copy in ctx_copies:
        copy.wait()
    count, near, act = flag_terms(
        horizons, windows, core_ref[0, 2], core_ref[0, 3], flags_ref[...]
    )
    stacked_dot(odd_ctx[frames : 3 * frames], weights, odd_pred)
    for copy in code_copies:
        copy.wait()
    shape = (horizons * frames, frames)
    row = lax.broadcasted_iota(jnp.int32, shape, 0)
    ahead = row % frames + row // frames + 1
    col = lax.broadcasted_iota(jnp.int32, shape, 1)
    here, after = col == ahead, col == ahead - frames
    preds = {-2: preds_ref[0], -1: odd_pred[0], 0: preds_ref[1], 1: odd_pred[1], 2: preds_ref[2]}
    factor = (1.0 / jnp.maximum(count, 1.0)) * scale
    beside = (-2, -1, 1, 2)
    for window in (-2, -1, 1, 2, 0):
        base = (window + 3) * frames
        query = preds[window]
        scores = rows_dot(query, codes[base : base + 5 * frames]) * scale
        block = {
            d: scores[:, (d + 2) * frames : (d + 3) * frames] for d in range(-REACH, REACH + 1)
        }
        positive = jnp.sum(
            jnp.where(here, block[0], 0.0) + jnp.where(after, block[1], 0.0),
            axis=1,
            keepdims=True,
        )
        for d in beside:
            usable = near[window + d + 4 : window + d + 5]
            block[d] = jnp.where(usable > 0, block[d], -1e30)
        top = jnp.maximum(jnp.maximum(block[-2], block[-1]), jnp.maximum(block[1], block[2]))
        top = jnp.maximum(positive, jnp.max(top, axis=1, keepdims=True))
        total = sum(jnp.exp(block[d] - top) for d in beside)
        total = jnp.sum(total, axis=1, keepdims=True)
        log_total = top + jnp.log(jnp.exp(positive - top) + total)
        active = act[:, window + 2 : window + 3]
        weight = factor * active
        pos_coef = weight * (jnp.exp(positive - log_total) - 1.0)
        pos_after = jnp.where(after, pos_coef, 0.0).astype(BF16)
        if window != 0:
            coef = (weight * jnp.exp(block[-window] - log_total)).astype(BF16)
            term = cols_dot(coef, query)
            if window == -1:
                term = term + cols_dot(pos_after, query)
            if window == -2:
                code_acc[...] = term
            else:
                code_acc[...] += term
        else:
            coefs = {d: (weight * jnp.exp(block[d] - log_total)).astype(BF16) for d in beside}
            coefs[0] = jnp.where(here, pos_coef, 0.0).astype(BF16)
            wide = jnp.concatenate([coefs[d] for d in range(-REACH, REACH + 1)], axis=1)
            delta = jnp.dot(
                wide, codes[base : base + 5 * frames], preferred_element_type=F32
            ) + jnp.dot(
                pos_after, codes[base + 3 * frames : base + 4 * frames], preferred_element_type=F32
            )
            delta = delta.astype(BF16)
            for part in range(parts):
                step, at = divmod(part * pred_cols, width)
                blocks[part // cores, part % cores, :, :pred_cols] = delta[
                    step * frames : (step + 1) * frames, at : at + pred_cols
                ]
            code_delta = (code_acc[...] + cols_dot(coefs[0], query)).astype(BF16)
            for part in range(parts):
                blocks[part // cores, part % cores, :, pred_cols:] = code_delta[
                    :, part * code_cols : (part + 1) * code_cols
                ]
            loss = jnp.sum(active * (log_total - positive), axis=0, keepdims=True)
            loss = loss * (1.0 / jnp.maximum(count, 1.0))
            loss_ref[...] = jnp.broadcast_to(loss, loss_ref.shape)
    for back, out in enumerate((out_0, out_1, out_2, out_3)):
        out[...] = blocks[(place + ring - back) % ring]


def term_kernel(
    pred_cols, core_ref, loss_ref, same_0, same_1, same_2, same_3, cross_0, cross_1, cross_2, cross_3,
    rows_same, rows_cross, out_ref, held,
):
    _, frames, lanes_all = same_0.shape
    plane = out_ref.shape[0]
    core, place = core_ref[0, 0], core_ref[0, 1]
    both = ((same_0, same_1, same_2, same_3), (cross_0, cross_1, cross_2, cross_3))
    ring = len(both[0])
    for side, blocks in enumerate(both):
        for spot, block in enumerate(blocks):
            start = pl.multiple_of((place + spot) % ring * frames, frames)
            held[side, pl.ds(start, frames)] = block[core]
    width = rows_same.shape[1] // 2
    rows = 2 * width // ring
    span = rows // plane
    depth = ring * span // 2
    for first, lanes in ((width, slice(0, pred_cols)), (0, slice(pred_cols, lanes_all))):
        for half in range(ring // 2):
            blocks = slice(first + half * rows, first + (half + 1) * rows)
            term = cols_dot(rows_same[:, blocks], held[0, :, lanes])
            term = term + cols_dot(rows_cross[:, blocks], held[1, :, lanes])
            term = term.reshape(2, plane, span // 2, -1)
            term = jnp.concatenate([term[0], term[1]], axis=1).astype(BF16)
            for tile in range(term.shape[2] // 128):
                at = (lanes.start // 128 + tile) * depth + half * span
                out_ref[:, at : at + span] = term[:, :, tile * 128 : (tile + 1) * 128]
    loss = loss_ref[...]
    high = loss.astype(BF16).astype(F32)
    middle = (loss - high).astype(BF16).astype(F32)
    row = lax.broadcasted_iota(jnp.int32, (16, 128), 0)
    terms = jnp.where(row == 0, high, jnp.where(row == 1, middle, loss - high - middle))
    terms = jnp.where(row < 3, terms, 0.0).astype(BF16)
    out_ref[:, out_ref.shape[1] - 16 :] = jnp.broadcast_to(terms[None], (plane, 16, 128))


def sum_kernel(core_ref, terms_ref, out_0, out_1, out_2, out_3, blocks):
    total = terms_ref[0].astype(F32)
    for source in range(1, terms_ref.shape[0]):
        total = total + terms_ref[source].astype(F32)
    place = core_ref[0, 1]
    ring, cores, rows, lanes = blocks.shape
    owned = rows // 2
    depth = ring * cores * owned
    loss = jnp.sum(total[total.shape[0] - 16 :, :1], axis=0, keepdims=True)
    for part in range(ring * cores):
        for tile in range(lanes // 128):
            at = tile * depth + part * owned
            blocks[part // cores, part % cores, :owned, tile * 128 : (tile + 1) * 128] = total[
                at : at + owned
            ]
        blocks[part // cores, part % cores, owned:] = jnp.broadcast_to(loss, (owned, lanes))
    for back, out in enumerate((out_0, out_1, out_2, out_3)):
        out[...] = blocks[(place + ring - back) % ring]


def gather_kernel(
    core_ref, same_0, same_1, same_2, same_3, cross_0, cross_1, cross_2, cross_3,
    loss_ref, pred_ref, proj_ref, held,
):
    core, place = core_ref[0, 0], core_ref[0, 1]
    both = ((same_0, same_1, same_2, same_3), (cross_0, cross_1, cross_2, cross_3))
    ring = len(both[0])
    for side, blocks in enumerate(both):
        for spot, block in enumerate(blocks):
            source = 2 * ((place + spot) % ring) + (core if side == 0 else 1 - core)
            held[source] = block[core]
    parts, rows, lanes = held.shape
    owned, horizons, width = pred_ref.shape
    code_cols = width // parts
    pred_cols = lanes - code_cols
    loss = jnp.zeros((1, 1), F32)
    for part in range(parts):
        block = held[part]
        step, at = divmod(part * pred_cols, width)
        pred_ref[:, step, at : at + pred_cols] = block[:owned, :pred_cols]
        proj_ref[:, part * code_cols : (part + 1) * code_cols] = block[:owned, pred_cols:]
        loss = loss + block[owned : owned + 1, :1]
    loss_ref[...] = loss


def per_device(features, context, predictor, projection, lengths, frame_mask):
    frames, width = features.shape[1], features.shape[2]
    horizons = predictor.shape[1]
    feat, ctx = features[0], context[0]
    windows, recordings = size_of(TM), size_of(DP)
    devices = windows * recordings
    parts, plane = size_of(RING), size_of(PLANE)
    tm = lax.axis_index(TM)
    core = lax.axis_index("core")

    encoded = jnp.dot(feat, projection, preferred_element_type=F32).astype(BF16)
    both = jnp.concatenate([encoded, ctx], axis=0)
    low2, high2 = window_at(both, -2), window_at(both, 2)
    both_x = other_core(both)
    positions = lax.broadcasted_iota(jnp.int32, (1, frames), 1)
    usable = ((frame_mask == 1) & (positions < lengths)).astype(F32)
    usable_x = other_core(usable)
    pair = jnp.concatenate(
        [jnp.where(core == 0, usable, usable_x), jnp.where(core == 0, usable_x, usable)], axis=1
    )
    pair, both_x = lax.optimization_barrier((pair, both_x))
    chips = size_of(CHIPS)
    flags = lax.all_to_all(
        jnp.broadcast_to(pair, (chips, 2 * frames)), CHIPS, 0, 0, tiled=True
    )
    low4, high4 = window_at(encoded, -4), window_at(encoded, 4)
    weights = predictor.reshape(width, horizons * width)
    low2, high2, weights, flags = lax.optimization_barrier((low2, high2, weights, flags))
    low2_x, high2_x = other_core(low2), other_core(high2)
    low4_x, high4_x = other_core(low4), other_core(high4)
    rows_ring = lax.all_gather(jnp.concatenate([feat, ctx], axis=1), "y", tiled=True)

    smem = pl.BlockSpec(memory_space=pltpu.SMEM)
    vmem = pl.BlockSpec(memory_space=pltpu.VMEM)
    anywhere = pl.BlockSpec(memory_space=pl.ANY)
    limit = pltpu.CompilerParams(vmem_limit_bytes=16 * 2**20)

    preds, done = pl.pallas_call(
        pred_kernel,
        out_shape=(
            jax.ShapeDtypeStruct((3, horizons * frames, width), BF16),
            jax.ShapeDtypeStruct((1, 128), F32),
        ),
        in_specs=[anywhere] * 3 + [vmem],
        out_specs=(vmem, vmem),
        scratch_shapes=[pltpu.VMEM((3 * frames, width), BF16), pltpu.SemaphoreType.DMA((3,))],
        compiler_params=limit,
        cost_estimate=pl.CostEstimate(flops=1600000000, bytes_accessed=6500000, transcendentals=0),
    )(low2, ctx, high2, weights)

    _, later = lax.optimization_barrier((done, rows_ring))
    rows_cross = other_core(later)

    pred_cols, code_cols = horizons * width // parts, width // parts
    lanes = pred_cols + code_cols
    core_word = jnp.stack([core, lax.axis_index("y"), lax.axis_index(ALL), tm])
    core_word = core_word.reshape(1, 4).astype(jnp.int32)
    ring = lax.axis_size("y")
    *deltas, loss_part = pl.pallas_call(
        functools.partial(delta_kernel, horizons, windows),
        out_shape=[jax.ShapeDtypeStruct((2, frames, lanes), BF16)] * ring
        + [jax.ShapeDtypeStruct((1, 128), F32)],
        in_specs=[smem] + [vmem] * 3 + [anywhere] * 10,
        out_specs=[vmem] * (ring + 1),
        scratch_shapes=[
            pltpu.VMEM((11 * frames, width), BF16),
            pltpu.VMEM((frames, width), F32),
            pltpu.VMEM((4 * frames, width), BF16),
            pltpu.VMEM((2, horizons * frames, width), BF16),
            pltpu.VMEM((ring, 2, frames, lanes), BF16),
            pltpu.SemaphoreType.DMA((13,)),
        ],
        compiler_params=pltpu.CompilerParams(vmem_limit_bytes=20 * 2**20),
        cost_estimate=pl.CostEstimate(
            flops=4000000000, bytes_accessed=12000000, transcendentals=900000
        ),
    )(
        core_word, flags, preds, weights,
        both, low2, high2, low4, high4, both_x, low2_x, high2_x, low4_x, high4_x,
    )

    _, rows_ring = lax.optimization_barrier((loss_part, rows_ring))
    rows_cross = other_core(rows_ring)
    same = [deltas[0]] + [ring_shift(deltas[step], ("y",), step) for step in range(1, ring)]
    cross = [other_core(block) for block in same]
    terms = pl.pallas_call(
        functools.partial(term_kernel, pred_cols),
        out_shape=jax.ShapeDtypeStruct((plane, width // plane * lanes // 128 + 16, 128), BF16),
        in_specs=[smem] + [vmem] * 11,
        out_specs=vmem,
        scratch_shapes=[pltpu.VMEM((2, ring * frames, lanes), BF16)],
        compiler_params=limit,
        cost_estimate=pl.CostEstimate(flops=1600000000, bytes_accessed=6000000, transcendentals=0),
    )(core_word, loss_part, *same, *cross, rows_ring, rows_cross)

    owned = width // devices
    terms = lax.all_to_all(terms, PLANE, 0, 0, tiled=True)
    block = jax.ShapeDtypeStruct((2, 2 * owned, lanes), F32)
    sums = pl.pallas_call(
        sum_kernel,
        out_shape=[block] * ring,
        in_specs=[smem, vmem],
        out_specs=[vmem] * ring,
        scratch_shapes=[pltpu.VMEM((ring, 2, 2 * owned, lanes), F32)],
    )(core_word, terms)
    same = [sums[0]] + [ring_shift(sums[step], ("y",), step) for step in range(1, ring)]
    cross = [other_core(block) for block in same]
    loss, grad_pred, grad_proj = pl.pallas_call(
        gather_kernel,
        out_shape=(
            jax.ShapeDtypeStruct((1, 1), F32),
            jax.ShapeDtypeStruct((owned, horizons, width), F32),
            jax.ShapeDtypeStruct((owned, width), F32),
        ),
        in_specs=[smem] + [vmem] * 8,
        out_specs=(vmem, vmem, vmem),
        scratch_shapes=[pltpu.VMEM((parts, 2 * owned, lanes), F32)],
    )(core_word, *same, *cross)
    return (loss.reshape(()), grad_pred, grad_proj)


def solution(mesh):
    fine = Mesh(mesh.devices.reshape(4, 2, 8, 2, 2), ALL)
    placed = (P(DP, TM, None), P(DP, TM, None), P(), P(), P(DP, TM), P(DP, TM))
    return jax.shard_map(
        per_device,
        mesh=fine,
        in_specs=placed,
        out_specs=(P(), P(ALL, None, None), P(ALL, None)),
        check_vma=False,
    )
```

profile of v0, /device:TPU:1, one launch (start us, length us, event | category | flops | bytes accessed | tf_op | source)
XLA Modules:
  0.0 139.6 jit_solution(16759096005487838203)
XLA Ops:
  7.2 2.0 %pad_maximum_fusion.1 = bf16[128,2048]{1,0:T(8,128)(2,1)} fusion(bf16[128,1024]{1,0:T(8,128)(2,1)} %bitcast.23, bf16[128,1024]{1,0:T(8,128)(2,1)} %bitcast.28), kind=kLoop, calls=%fused_computation.2 | loop fusion | flops 1048576 | bytes 1048576 | tf_op jit(solution)/shard_map/concatenate | solution.py:338
  9.3 1.4 %convolution_convert_fusion = bf16[128,1024]{1,0:T(8,128)(2,1)S(1)} fusion(bf16[1024,1024]{1,0:T(8,128)(2,1)S(1)} %copy-done, bf16[1,128,1024]{2,1,0:T(8,128)(2,1)} %param.6), kind=kOutput, calls=%fused_computation | convolution fusion | flops 268566528 | bytes 2621440 | tf_op jit(solution)/shard_map/dot_general | solution.py:318
  10.8 3.3 %collective-permute-start.3 = (bf16[256,1024]{1,0:T(8,128)(2,1)S(1)}, bf16[256,1024]{1,0:T(8,128)(2,1)S(1)}, u32[]{:S(2)}, u32[]{:S(2)}) collective-permute-start(bf16[256,1024]{1,0:T(8,128)(2,1)S(1)} %pad_maximum_fusion.both), channel_id=1, source_target_pairs={{0,1},{1,0},{2,3},{3,2},{4,5},{5,4},{6,7},{7,6},{8,9},{9,8},{10,11... | collective-permute-start | bytes 1572872 | tf_op jit(solution)/shard_map/ppermute | solution.py:38
  14.8 0.1 collective-permute-start.2
  14.9 0.1 collective-permute-start
  15.0 4.8 %collective-permute-start.1 = (bf16[256,1024]{1,0:T(8,128)(2,1)S(1)}, bf16[256,1024]{1,0:T(8,128)(2,1)}, u32[]{:S(2)}, u32[]{:S(2)}) collective-permute-start(bf16[256,1024]{1,0:T(8,128)(2,1)S(1)} %pad_maximum_fusion.both), channel_id=1, source_target_pairs={{2,0},{3,1},{4,2},{5,3},{6,4},{7,5},{8,6},{9,7},{10,8},{11,9},{12,... | collective-permute-start | bytes 1572872 | tf_op jit(solution)/shard_map/ppermute | solution.py:30
  19.9 0.7 broadcast_in_dim.2
  20.6 13.0 %all-to-all-start = ((f32[128,1,256]{2,1,0:T(1,128)}), f32[128,1,256]{2,1,0:T(1,128)}, u32[]{:S(2)}, u32[]{:S(2)}) async-start(f32[128,1,256]{2,1,0:T(1,128)} %broadcast_in_dim.2), calls=%async_computation | async-start | bytes 262144 | tf_op jit(solution)/shard_map/all_to_all | solution.py:330
  33.6 0.6 collective-permute-start.4
  34.2 2.2 %collective-permute-start.5 = (bf16[128,1024]{1,0:T(8,128)(2,1)}, bf16[128,1024]{1,0:T(8,128)(2,1)}, u32[]{:S(2)}, u32[]{:S(2)}) collective-permute-start(bf16[128,1024]{1,0:T(8,128)(2,1)} %copy-done.9), channel_id=1, source_target_pairs={{4,0},{5,1},{6,2},{7,3},{8,4},{9,5},{10,6},{11,7},{12,8},{13,9},{1... | collective-permute-start | bytes 786440 | tf_op jit(solution)/shard_map/ppermute | solution.py:30
  36.4 5.6 %copy.10 = bf16[128,8,2,1024]{3,1,2,0:T(8,128)(2,1)} copy(bf16[128,8,2,1024]{3,2,1,0:T(2,128)(2,1)} %bitcast.27) | data formatting | bytes 8388608
  42.0 2.4 %all-to-all-done = f32[128,1,256]{2,1,0:T(1,128)} async-done(((f32[128,1,256]{2,1,0:T(1,128)}), f32[128,1,256]{2,1,0:T(1,128)}, u32[]{:S(2)}, u32[]{:S(2)}) %all-to-all-start) | async-done | bytes 131104 | tf_op jit(solution)/shard_map/all_to_all | solution.py:330
  44.3 0.9 copy.12
  45.3 3.2 %collective-permute-start.6 = (bf16[256,1024]{1,0:T(8,128)(2,1)}, bf16[256,1024]{1,0:T(8,128)(2,1)}, u32[]{:S(2)}, u32[]{:S(2)}) collective-permute-start(bf16[256,1024]{1,0:T(8,128)(2,1)} %collective-permute-done.low2), channel_id=1, source_target_pairs={{0,1},{1,0},{2,3},{3,2},{4,5},{5,4},{6,7},{7,6},{8,9},{9,8},{10,11... | collective-permute-start | bytes 1572872 | tf_op jit(solution)/shard_map/ppermute | solution.py:38
  48.5 0.1 collective-permute-start.7
  48.6 0.4 collective-permute-start.8
  49.0 0.3 collective-permute-start.9
  49.4 2.2 %copy-done.1 = bf16[128,8,2,1024]{3,1,2,0:T(8,128)(2,1)S(1)} copy-done((bf16[128,8,2,1024]{3,1,2,0:T(8,128)(2,1)S(1)}, bf16[128,8,2,1024]{3,1,2,0:T(8,128)(2,1)}, u32[]{:S(2)}) %copy-start.1) | copy-done | bytes 4194328
  51.6 3.4 %shard_map.85 = (bf16[3,256,1024]{2,1,0:T(8,128)(2,1)S(1)}, f32[1,128]{1,0:T(1,128)}) custom-call(bf16[256,1024]{1,0:T(8,128)(2,1)} %collective-permute-done.low2, bf16[128,1024]{1,0:T(8,128)(2,1)S(1)} %bitcast.25, bf16[256,1024]{1,0:T(8,128)(2,1)} %collective-permute-done.1.high2, bf16[1024,2048]{1,0:T(8,128)(2,1)S(1)} %bitcast.21), custom_call_target="tpu_custom_call" | custom-call | flops 1600000000 | bytes 6500000 | tf_op jit(solution)/shard_map/pallas_call | solution.py:345
  55.0 8.8 %shard_map.86 = (bf16[2,128,384]{2,1,0:T(8,128)(2,1)S(1)}, bf16[2,128,384]{2,1,0:T(8,128)(2,1)S(1)}, bf16[2,128,384]{2,1,0:T(8,128)(2,1)S(1)}, bf16[2,128,384]{2,1,0:T(8,128)(2,1)S(1)}, f32[1,128]{1,0:T(1,128)S(1)}) custom-call(s32[1,4]{1,0:T(1,128)S(1)} %add_bitcast_fusion.core_ref, f32[128,256]{1,0:T(8,128)S(1)} %bitcast.26, ...), custom_call_target="tpu_custom_call" | custom-call | flops 4000000000 | bytes 12000000 | tf_op jit(solution)/shard_map/pallas_call | solution.py:366
  63.9 0.7 copy-done.6
  64.5 0.7 copy-done.7
  65.2 0.7 copy-done.8
  65.9 0.2 collective-permute-start.17
  66.2 0.7 collective-permute-start.10
  66.8 1.5 %collective-permute-start.11 = (bf16[2,128,384]{2,1,0:T(8,128)(2,1)}, bf16[2,128,384]{2,1,0:T(8,128)(2,1)S(1)}, u32[]{:S(2)}, u32[]{:S(2)}) collective-permute-start(bf16[2,128,384]{2,1,0:T(8,128)(2,1)} %copy-done.7), channel_id=1, source_target_pairs={{128,0},{192,64},{0,128},{64,192},{129,1},{193,65},{1,129},{65,193... | collective-permute-start | bytes 589832 | tf_op jit(solution)/shard_map/ppermute | solution.py:30
  68.3 0.8 collective-permute-start.13
  69.1 3.5 %collective-permute-done.10.same_1 = bf16[2,128,384]{2,1,0:T(8,128)(2,1)S(1)} collective-permute-done((bf16[2,128,384]{2,1,0:T(8,128)(2,1)}, bf16[2,128,384]{2,1,0:T(8,128)(2,1)S(1)}, u32[]{:S(2)}, u32[]{:S(2)}) %collective-permute-start.10) | collective-permute-done | bytes 196640 | tf_op jit(solution)/shard_map/ppermute | solution.py:30
  72.6 1.8 %collective-permute-start.14 = (bf16[2,128,384]{2,1,0:T(8,128)(2,1)S(1)}, bf16[2,128,384]{2,1,0:T(8,128)(2,1)S(1)}, u32[]{:S(2)}, u32[]{:S(2)}) collective-permute-start(bf16[2,128,384]{2,1,0:T(8,128)(2,1)S(1)} %collective-permute-done.10.same_1), channel_id=1, source_target_pairs={{0,1},{1,0},{2,3},{3,2},{4,5},{5,4},{6,7},{7,6},{8,9},{9,8},{10,11... | collective-permute-start | bytes 589832 | tf_op jit(solution)/shard_map/ppermute | solution.py:38
  74.4 0.1 collective-permute-done.11.same_2
  74.5 2.4 %collective-permute-start.15 = (bf16[2,128,384]{2,1,0:T(8,128)(2,1)S(1)}, bf16[2,128,384]{2,1,0:T(8,128)(2,1)S(1)}, u32[]{:S(2)}, u32[]{:S(2)}) collective-permute-start(bf16[2,128,384]{2,1,0:T(8,128)(2,1)S(1)} %collective-permute-done.11.same_2), channel_id=1, source_target_pairs={{0,1},{1,0},{2,3},{3,2},{4,5},{5,4},{6,7},{7,6},{8,9},{9,8},{10,11... | collective-permute-start | bytes 589832 | tf_op jit(solution)/shard_map/ppermute | solution.py:38
  76.9 2.7 %collective-permute-done.12.same_3 = bf16[2,128,384]{2,1,0:T(8,128)(2,1)S(1)} collective-permute-done((bf16[2,128,384]{2,1,0:T(8,128)(2,1)}, bf16[2,128,384]{2,1,0:T(8,128)(2,1)S(1)}, u32[]{:S(2)}, u32[]{:S(2)}) %collective-permute-start.12) | collective-permute-done | bytes 196640 | tf_op jit(solution)/shard_map/ppermute | solution.py:30
  79.6 0.5 collective-permute-start.16
  80.1 1.1 collective-permute-done.16.cross_3
  81.2 1.6 %copy-done.3 = bf16[512,2048]{1,0:T(8,128)(2,1)S(1)} copy-done((bf16[512,2048]{1,0:T(8,128)(2,1)S(1)}, bf16[512,2048]{1,0:T(8,128)(2,1)}, u32[]{:S(2)}) %copy-start.3) | copy-done | bytes 2097176
  82.8 1.9 %shard_map.87 = bf16[32,112,128]{2,1,0:T(8,128)(2,1)S(1)} custom-call(s32[1,4]{1,0:T(1,128)S(1)} %add_bitcast_fusion.core_ref, f32[1,128]{1,0:T(1,128)S(1)} %get-tuple-element.30.loss_ref, bf16[2,128,384]{2,1,0:T(8,128)(2,1)S(1)} %get-tuple-element.31.same_0, bf16[2,128,384]{2,1,0:T(8,128)(2,1)S(1)} %collective-permute-done.10.same_1, ...), custom_call_target="tpu_custom_call" | custom-call | flops 1600000000 | bytes 6000000 | tf_op jit(solution)/shard_map/pallas_call | solution.py:393
  84.6 32.5 %all_to_all.14.terms_ref = bf16[32,112,128]{2,1,0:T(8,128)(2,1)} all-to-all(bf16[32,112,128]{2,1,0:T(8,128)(2,1)S(1)} %shard_map.87), channel_id=1, replica_groups=mesh['y'=4,'xh'=2,'z'=8,'xl'=2,'core'=2] {'xh','z','xl'}, dimensions={0} | all-to-all | bytes 1835008 | tf_op jit(solution)/shard_map/all_to_all | solution.py:404
  117.1 2.0 %shard_map.88 = (f32[2,8,384]{2,1,0:T(8,128)}, f32[2,8,384]{2,1,0:T(8,128)}, f32[2,8,384]{2,1,0:T(8,128)}, f32[2,8,384]{2,1,0:T(8,128)}) custom-call(s32[1,4]{1,0:T(1,128)} %copy-done.5, bf16[32,112,128]{2,1,0:T(8,128)(2,1)} %all_to_all.14.terms_ref), custom_call_target="tpu_custom_call" | custom-call | tf_op jit(solution)/shard_map/pallas_call | solution.py:406
  119.1 0.7 collective-permute-start.18
  119.8 1.0 collective-permute-start.19
  120.8 0.5 collective-permute-start.20
  121.4 4.0 %collective-permute-start.21 = (f32[2,8,384]{2,1,0:T(8,128)}, f32[2,8,384]{2,1,0:T(8,128)S(1)}, u32[]{:S(2)}, u32[]{:S(2)}) collective-permute-start(f32[2,8,384]{2,1,0:T(8,128)} %get-tuple-element.36.same_0), channel_id=1, source_target_pairs={{0,1},{1,0},{2,3},{3,2},{4,5},{5,4},{6,7},{7,6},{8,9},{9,8},{10,11... | collective-permute-start | bytes 73736 | tf_op jit(solution)/shard_map/ppermute | solution.py:38
  125.3 0.9 collective-permute-start.22
  126.2 2.3 %collective-permute-start.23 = (f32[2,8,384]{2,1,0:T(8,128)S(1)}, f32[2,8,384]{2,1,0:T(8,128)S(1)}, u32[]{:S(2)}, u32[]{:S(2)}) collective-permute-start(f32[2,8,384]{2,1,0:T(8,128)S(1)} %collective-permute-done.19.same_2), channel_id=1, source_target_pairs={{0,1},{1,0},{2,3},{3,2},{4,5},{5,4},{6,7},{7,6},{8,9},{9,8},{10,11... | collective-permute-start | bytes 73736 | tf_op jit(solution)/shard_map/ppermute | solution.py:38
  128.5 1.2 collective-permute-start.24
  129.8 0.8 collective-permute-done.24.cross_3
  130.6 0.6 copy-done.16
  131.2 1.5 %shard_map.89 = (f32[1,1]{1,0:T(1,128)}, f32[4,2,1024]{2,1,0:T(2,128)}, f32[4,1024]{1,0:T(4,128)}) custom-call(s32[1,4]{1,0:T(1,128)} %copy-done.5, f32[2,8,384]{2,1,0:T(8,128)} %get-tuple-element.36.same_0, f32[2,8,384]{2,1,0:T(8,128)} %copy-done.10, f32[2,8,384]{2,1,0:T(8,128)} %copy-done.11, f32[2,8,384]{2,1,0:T(8,128)} %copy-done.12, ...), custom_call_target="tpu_custom_call" | custom-call | tf_op jit(solution)/shard_map/pallas_call | solution.py:415
  (59 shorter events, 0.3 us)
Async XLA Ops:
  7.2 2.1 %copy-start = (bf16[1024,1024]{1,0:T(8,128)(2,1)S(1)}, bf16[1024,1024]{1,0:T(8,128)(2,1)}, u32[]{:S(2)}) copy-start(bf16[1024,1024]{1,0:T(8,128)(2,1)} %param.9) | copy-start | bytes 6291460
  7.2 58.7 %all-gather.2.cloned.1.call-start = ((), (), s32[]{:S(2)}) async-start(), calls=%async_computation.2 | async-start | bytes 2621440 | tf_op jit(solution)/shard_map/all_gather | solution.py:338
  7.2 3.5 %copy-start.4 = (bf16[1,128,1024]{2,1,0:T(8,128)(2,1)S(1)}, bf16[1,128,1024]{2,1,0:T(8,128)(2,1)}, u32[]{:S(2)}) copy-start(bf16[1,128,1024]{2,1,0:T(8,128)(2,1)} %param.7) | copy-start | bytes 786436
  9.3 5.5 %copy-start.17 = (s32[1,128]{1,0:T(1,128)S(1)}, s32[1,128]{1,0:T(1,128)}, u32[]{:S(2)}) copy-start(s32[1,128]{1,0:T(1,128)} %param.11) | copy-start | bytes 1540
  10.7 4.2 %copy-start.9 = (bf16[128,1024]{1,0:T(8,128)(2,1)}, bf16[128,1024]{1,0:T(8,128)(2,1)S(1)}, u32[]{:S(2)}) copy-start(bf16[128,1024]{1,0:T(8,128)(2,1)S(1)} %convolution_convert_fusion) | copy-start | bytes 786436
  10.8 9.1 %collective-permute-start.3 = (bf16[256,1024]{1,0:T(8,128)(2,1)S(1)}, bf16[256,1024]{1,0:T(8,128)(2,1)S(1)}, u32[]{:S(2)}, u32[]{:S(2)}) collective-permute-start(bf16[256,1024]{1,0:T(8,128)(2,1)S(1)} %pad_maximum_fusion.both), channel_id=1, source_target_pairs={{0,1},{1,0},{2,3},{3,2},{4,5},{5,4},{6,7},{7,6},{8,9},{9,8},{10,11... | collective-permute-start | bytes 1572872 | tf_op jit(solution)/shard_map/ppermute | solution.py:38
  14.8 5.1 %collective-permute-start.2 = (f32[1,128]{1,0:T(1,128)S(1)}, f32[1,128]{1,0:T(1,128)S(1)}, u32[]{:S(2)}, u32[]{:S(2)}) collective-permute-start(f32[1,128]{1,0:T(1,128)S(1)} %and_convert_fusion), channel_id=1, source_target_pairs={{0,1},{1,0},{2,3},{3,2},{4,5},{5,4},{6,7},{7,6},{8,9},{9,8},{10,11... | collective-permute-start | bytes 1544 | tf_op jit(solution)/shard_map/ppermute | solution.py:38
  14.9 30.4 %collective-permute-start = (bf16[256,1024]{1,0:T(8,128)(2,1)S(1)}, bf16[256,1024]{1,0:T(8,128)(2,1)}, u32[]{:S(2)}, u32[]{:S(2)}) collective-permute-start(bf16[256,1024]{1,0:T(8,128)(2,1)S(1)} %pad_maximum_fusion.both), channel_id=1, source_target_pairs={{30,0},{31,1},{0,2},{1,3},{2,4},{3,5},{4,6},{5,7},{6,8},{7,9},{8,1... | collective-permute-start | bytes 1572872 | tf_op jit(solution)/shard_map/ppermute | solution.py:30
  15.0 30.3 %collective-permute-start.1 = (bf16[256,1024]{1,0:T(8,128)(2,1)S(1)}, bf16[256,1024]{1,0:T(8,128)(2,1)}, u32[]{:S(2)}, u32[]{:S(2)}) collective-permute-start(bf16[256,1024]{1,0:T(8,128)(2,1)S(1)} %pad_maximum_fusion.both), channel_id=1, source_target_pairs={{2,0},{3,1},{4,2},{5,3},{6,4},{7,5},{8,6},{9,7},{10,8},{11,9},{12,... | collective-permute-start | bytes 1572872 | tf_op jit(solution)/shard_map/ppermute | solution.py:30
  20.6 23.8 %all-to-all-start = ((f32[128,1,256]{2,1,0:T(1,128)}), f32[128,1,256]{2,1,0:T(1,128)}, u32[]{:S(2)}, u32[]{:S(2)}) async-start(f32[128,1,256]{2,1,0:T(1,128)} %broadcast_in_dim.2), calls=%async_computation | async-start | bytes 262144 | tf_op jit(solution)/shard_map/all_to_all | solution.py:330
  33.6 15.0 %collective-permute-start.4 = (bf16[128,1024]{1,0:T(8,128)(2,1)}, bf16[128,1024]{1,0:T(8,128)(2,1)}, u32[]{:S(2)}, u32[]{:S(2)}) collective-permute-start(bf16[128,1024]{1,0:T(8,128)(2,1)} %copy-done.9), channel_id=1, source_target_pairs={{28,0},{29,1},{30,2},{31,3},{0,4},{1,5},{2,6},{3,7},{4,8},{5,9},{6... | collective-permute-start | bytes 786440 | tf_op jit(solution)/shard_map/ppermute | solution.py:30
  34.2 14.8 %collective-permute-start.5 = (bf16[128,1024]{1,0:T(8,128)(2,1)}, bf16[128,1024]{1,0:T(8,128)(2,1)}, u32[]{:S(2)}, u32[]{:S(2)}) collective-permute-start(bf16[128,1024]{1,0:T(8,128)(2,1)} %copy-done.9), channel_id=1, source_target_pairs={{4,0},{5,1},{6,2},{7,3},{8,4},{9,5},{10,6},{11,7},{12,8},{13,9},{1... | collective-permute-start | bytes 786440 | tf_op jit(solution)/shard_map/ppermute | solution.py:30
  45.3 9.7 %collective-permute-start.6 = (bf16[256,1024]{1,0:T(8,128)(2,1)}, bf16[256,1024]{1,0:T(8,128)(2,1)}, u32[]{:S(2)}, u32[]{:S(2)}) collective-permute-start(bf16[256,1024]{1,0:T(8,128)(2,1)} %collective-permute-done.low2), channel_id=1, source_target_pairs={{0,1},{1,0},{2,3},{3,2},{4,5},{5,4},{6,7},{7,6},{8,9},{9,8},{10,11... | collective-permute-start | bytes 1572872 | tf_op jit(solution)/shard_map/ppermute | solution.py:38
  48.5 6.5 %collective-permute-start.7 = (bf16[256,1024]{1,0:T(8,128)(2,1)}, bf16[256,1024]{1,0:T(8,128)(2,1)}, u32[]{:S(2)}, u32[]{:S(2)}) collective-permute-start(bf16[256,1024]{1,0:T(8,128)(2,1)} %collective-permute-done.1.high2), channel_id=1, source_target_pairs={{0,1},{1,0},{2,3},{3,2},{4,5},{5,4},{6,7},{7,6},{8,9},{9,8},{10,11... | collective-permute-start | bytes 1572872 | tf_op jit(solution)/shard_map/ppermute | solution.py:38
  48.6 6.4 %collective-permute-start.8 = (bf16[128,1024]{1,0:T(8,128)(2,1)}, bf16[128,1024]{1,0:T(8,128)(2,1)S(1)}, u32[]{:S(2)}, u32[]{:S(2)}) collective-permute-start(bf16[128,1024]{1,0:T(8,128)(2,1)} %collective-permute-done.4.low4), channel_id=1, source_target_pairs={{0,1},{1,0},{2,3},{3,2},{4,5},{5,4},{6,7},{7,6},{8,9},{9,8},{10,11... | collective-permute-start | bytes 786440 | tf_op jit(solution)/shard_map/ppermute | solution.py:38
  49.0 6.0 %collective-permute-start.9 = (bf16[128,1024]{1,0:T(8,128)(2,1)}, bf16[128,1024]{1,0:T(8,128)(2,1)S(1)}, u32[]{:S(2)}, u32[]{:S(2)}) collective-permute-start(bf16[128,1024]{1,0:T(8,128)(2,1)} %collective-permute-done.5.high4), channel_id=1, source_target_pairs={{0,1},{1,0},{2,3},{3,2},{4,5},{5,4},{6,7},{7,6},{8,9},{9,8},{10,11... | collective-permute-start | bytes 786440 | tf_op jit(solution)/shard_map/ppermute | solution.py:38
  49.4 2.2 %copy-start.1 = (bf16[128,8,2,1024]{3,1,2,0:T(8,128)(2,1)S(1)}, bf16[128,8,2,1024]{3,1,2,0:T(8,128)(2,1)}, u32[]{:S(2)}) copy-start(bf16[128,8,2,1024]{3,1,2,0:T(8,128)(2,1)} %copy.10) | copy-start | bytes 12582916
  51.6 29.6 %copy-start.5 = (s32[1,4]{1,0:T(1,128)}, s32[1,4]{1,0:T(1,128)S(1)}, u32[]{:S(2)}) copy-start(s32[1,4]{1,0:T(1,128)S(1)} %add_bitcast_fusion.core_ref) | copy-start | bytes 52
  51.6 3.5 %copy-start.2 = (bf16[128,8,2,1024]{3,1,2,0:T(8,128)(2,1)S(1)}, bf16[128,8,2,1024]{3,1,2,0:T(8,128)(2,1)}, u32[]{:S(2)}) copy-start(bf16[128,8,2,1024]{3,1,2,0:T(8,128)(2,1)} %copy.10) | copy-start | bytes 12582916
  63.9 0.7 copy-start.6
  64.5 0.7 copy-start.7
  65.2 0.7 copy-start.8
  65.9 15.2 %collective-permute-start.17 = (bf16[512,2048]{1,0:T(8,128)(2,1)}, bf16[512,2048]{1,0:T(8,128)(2,1)S(1)}, u32[]{:S(2)}, u32[]{:S(2)}) collective-permute-start(bf16[512,2048]{1,0:T(8,128)(2,1)} %all-gather.2.cloned.1.call-done.rows_same), channel_id=1, source_target_pairs={{0,1},{1,0},{2,3},{3,2},{4,5},{5,4},{6,7},{7,6},{8,9},{9,8},{10,11... | collective-permute-start | bytes 6291464 | tf_op jit(solution)/shard_map/ppermute | solution.py:38
  66.2 6.4 %collective-permute-start.10 = (bf16[2,128,384]{2,1,0:T(8,128)(2,1)}, bf16[2,128,384]{2,1,0:T(8,128)(2,1)S(1)}, u32[]{:S(2)}, u32[]{:S(2)}) collective-permute-start(bf16[2,128,384]{2,1,0:T(8,128)(2,1)} %copy-done.8), channel_id=1, source_target_pairs={{64,0},{128,64},{192,128},{0,192},{65,1},{129,65},{193,129},{1,193... | collective-permute-start | bytes 589832 | tf_op jit(solution)/shard_map/ppermute | solution.py:30
  66.8 7.7 %collective-permute-start.11 = (bf16[2,128,384]{2,1,0:T(8,128)(2,1)}, bf16[2,128,384]{2,1,0:T(8,128)(2,1)S(1)}, u32[]{:S(2)}, u32[]{:S(2)}) collective-permute-start(bf16[2,128,384]{2,1,0:T(8,128)(2,1)} %copy-done.7), channel_id=1, source_target_pairs={{128,0},{192,64},{0,128},{64,192},{129,1},{193,65},{1,129},{65,193... | collective-permute-start | bytes 589832 | tf_op jit(solution)/shard_map/ppermute | solution.py:30
  68.3 11.3 %collective-permute-start.12 = (bf16[2,128,384]{2,1,0:T(8,128)(2,1)}, bf16[2,128,384]{2,1,0:T(8,128)(2,1)S(1)}, u32[]{:S(2)}, u32[]{:S(2)}) collective-permute-start(bf16[2,128,384]{2,1,0:T(8,128)(2,1)} %copy-done.6), channel_id=1, source_target_pairs={{192,0},{0,64},{64,128},{128,192},{193,1},{1,65},{65,129},{129,193... | collective-permute-start | bytes 589832 | tf_op jit(solution)/shard_map/ppermute | solution.py:30
  68.3 11.8 %collective-permute-start.13 = (bf16[2,128,384]{2,1,0:T(8,128)(2,1)S(1)}, bf16[2,128,384]{2,1,0:T(8,128)(2,1)S(1)}, u32[]{:S(2)}, u32[]{:S(2)}) collective-permute-start(bf16[2,128,384]{2,1,0:T(8,128)(2,1)S(1)} %get-tuple-element.31.same_0), channel_id=1, source_target_pairs={{0,1},{1,0},{2,3},{3,2},{4,5},{5,4},{6,7},{7,6},{8,9},{9,8},{10,11... | collective-permute-start | bytes 589832 | tf_op jit(solution)/shard_map/ppermute | solution.py:38
  72.6 7.5 %collective-permute-start.14 = (bf16[2,128,384]{2,1,0:T(8,128)(2,1)S(1)}, bf16[2,128,384]{2,1,0:T(8,128)(2,1)S(1)}, u32[]{:S(2)}, u32[]{:S(2)}) collective-permute-start(bf16[2,128,384]{2,1,0:T(8,128)(2,1)S(1)} %collective-permute-done.10.same_1), channel_id=1, source_target_pairs={{0,1},{1,0},{2,3},{3,2},{4,5},{5,4},{6,7},{7,6},{8,9},{9,8},{10,11... | collective-permute-start | bytes 589832 | tf_op jit(solution)/shard_map/ppermute | solution.py:38
  74.5 5.6 %collective-permute-start.15 = (bf16[2,128,384]{2,1,0:T(8,128)(2,1)S(1)}, bf16[2,128,384]{2,1,0:T(8,128)(2,1)S(1)}, u32[]{:S(2)}, u32[]{:S(2)}) collective-permute-start(bf16[2,128,384]{2,1,0:T(8,128)(2,1)S(1)} %collective-permute-done.11.same_2), channel_id=1, source_target_pairs={{0,1},{1,0},{2,3},{3,2},{4,5},{5,4},{6,7},{7,6},{8,9},{9,8},{10,11... | collective-permute-start | bytes 589832 | tf_op jit(solution)/shard_map/ppermute | solution.py:38
  79.6 1.6 %collective-permute-start.16 = (bf16[2,128,384]{2,1,0:T(8,128)(2,1)S(1)}, bf16[2,128,384]{2,1,0:T(8,128)(2,1)S(1)}, u32[]{:S(2)}, u32[]{:S(2)}) collective-permute-start(bf16[2,128,384]{2,1,0:T(8,128)(2,1)S(1)} %collective-permute-done.12.same_3), channel_id=1, source_target_pairs={{0,1},{1,0},{2,3},{3,2},{4,5},{5,4},{6,7},{7,6},{8,9},{9,8},{10,11... | collective-permute-start | bytes 589832 | tf_op jit(solution)/shard_map/ppermute | solution.py:38
  81.2 1.6 %copy-start.3 = (bf16[512,2048]{1,0:T(8,128)(2,1)S(1)}, bf16[512,2048]{1,0:T(8,128)(2,1)}, u32[]{:S(2)}) copy-start(bf16[512,2048]{1,0:T(8,128)(2,1)} %all-gather.2.cloned.1.call-done.rows_same) | copy-start | bytes 6291460
  119.1 6.2 %collective-permute-start.18 = (f32[2,8,384]{2,1,0:T(8,128)}, f32[2,8,384]{2,1,0:T(8,128)S(1)}, u32[]{:S(2)}, u32[]{:S(2)}) collective-permute-start(f32[2,8,384]{2,1,0:T(8,128)} %get-tuple-element.37), channel_id=1, source_target_pairs={{64,0},{128,64},{192,128},{0,192},{65,1},{129,65},{193,129},{1,193... | collective-permute-start | bytes 73736 | tf_op jit(solution)/shard_map/ppermute | solution.py:30
  119.8 6.5 %collective-permute-start.19 = (f32[2,8,384]{2,1,0:T(8,128)}, f32[2,8,384]{2,1,0:T(8,128)S(1)}, u32[]{:S(2)}, u32[]{:S(2)}) collective-permute-start(f32[2,8,384]{2,1,0:T(8,128)} %get-tuple-element.38), channel_id=1, source_target_pairs={{128,0},{192,64},{0,128},{64,192},{129,1},{193,65},{1,129},{65,193... | collective-permute-start | bytes 73736 | tf_op jit(solution)/shard_map/ppermute | solution.py:30
  120.8 7.7 %collective-permute-start.20 = (f32[2,8,384]{2,1,0:T(8,128)}, f32[2,8,384]{2,1,0:T(8,128)S(1)}, u32[]{:S(2)}, u32[]{:S(2)}) collective-permute-start(f32[2,8,384]{2,1,0:T(8,128)} %get-tuple-element.39), channel_id=1, source_target_pairs={{192,0},{0,64},{64,128},{128,192},{193,1},{1,65},{65,129},{129,193... | collective-permute-start | bytes 73736 | tf_op jit(solution)/shard_map/ppermute | solution.py:30
  121.4 8.4 %collective-permute-start.21 = (f32[2,8,384]{2,1,0:T(8,128)}, f32[2,8,384]{2,1,0:T(8,128)S(1)}, u32[]{:S(2)}, u32[]{:S(2)}) collective-permute-start(f32[2,8,384]{2,1,0:T(8,128)} %get-tuple-element.36.same_0), channel_id=1, source_target_pairs={{0,1},{1,0},{2,3},{3,2},{4,5},{5,4},{6,7},{7,6},{8,9},{9,8},{10,11... | collective-permute-start | bytes 73736 | tf_op jit(solution)/shard_map/ppermute | solution.py:38
  125.3 5.3 %copy-start.10 = (f32[2,8,384]{2,1,0:T(8,128)}, f32[2,8,384]{2,1,0:T(8,128)S(1)}, u32[]{:S(2)}) copy-start(f32[2,8,384]{2,1,0:T(8,128)S(1)} %collective-permute-done.18.same_1) | copy-start | bytes 73732
  125.3 4.4 %collective-permute-start.22 = (f32[2,8,384]{2,1,0:T(8,128)S(1)}, f32[2,8,384]{2,1,0:T(8,128)S(1)}, u32[]{:S(2)}, u32[]{:S(2)}) collective-permute-start(f32[2,8,384]{2,1,0:T(8,128)S(1)} %collective-permute-done.18.same_1), channel_id=1, source_target_pairs={{0,1},{1,0},{2,3},{3,2},{4,5},{5,4},{6,7},{7,6},{8,9},{9,8},{10,11... | collective-permute-start | bytes 73736 | tf_op jit(solution)/shard_map/ppermute | solution.py:38
  126.2 4.4 %copy-start.11 = (f32[2,8,384]{2,1,0:T(8,128)}, f32[2,8,384]{2,1,0:T(8,128)S(1)}, u32[]{:S(2)}) copy-start(f32[2,8,384]{2,1,0:T(8,128)S(1)} %collective-permute-done.19.same_2) | copy-start | bytes 73732
  126.2 3.5 %collective-permute-start.23 = (f32[2,8,384]{2,1,0:T(8,128)S(1)}, f32[2,8,384]{2,1,0:T(8,128)S(1)}, u32[]{:S(2)}, u32[]{:S(2)}) collective-permute-start(f32[2,8,384]{2,1,0:T(8,128)S(1)} %collective-permute-done.19.same_2), channel_id=1, source_target_pairs={{0,1},{1,0},{2,3},{3,2},{4,5},{5,4},{6,7},{7,6},{8,9},{9,8},{10,11... | collective-permute-start | bytes 73736 | tf_op jit(solution)/shard_map/ppermute | solution.py:38
  128.5 2.1 %copy-start.12 = (f32[2,8,384]{2,1,0:T(8,128)}, f32[2,8,384]{2,1,0:T(8,128)S(1)}, u32[]{:S(2)}) copy-start(f32[2,8,384]{2,1,0:T(8,128)S(1)} %collective-permute-done.20.same_3) | copy-start | bytes 73732
  128.5 2.1 %collective-permute-start.24 = (f32[2,8,384]{2,1,0:T(8,128)S(1)}, f32[2,8,384]{2,1,0:T(8,128)S(1)}, u32[]{:S(2)}, u32[]{:S(2)}) collective-permute-start(f32[2,8,384]{2,1,0:T(8,128)S(1)} %collective-permute-done.20.same_3), channel_id=1, source_target_pairs={{0,1},{1,0},{2,3},{3,2},{4,5},{5,4},{6,7},{7,6},{8,9},{9,8},{10,11... | collective-permute-start | bytes 73736 | tf_op jit(solution)/shard_map/ppermute | solution.py:38
  129.7 0.9 copy-start.13
  129.8 0.9 copy-start.14
  129.8 0.8 copy-start.15
  130.6 0.6 copy-start.16
Sparse Core Ops, SparseCore 0:
  9.8 38.6 all-gather.1
where the time goes:
time: 140 us
  starting transfers between devices  46.7 us (33%)
  blocking collectives  32.5 us (23%)
  Pallas kernels  17.6 us (13%)
  between operations  15 us (11%)
  local copies, waits for them, and re-layouts  13.7 us (10%)
  waiting for transfers between devices  10.6 us (8%)
  other arithmetic  2.15 us (2%)
    all_to_all x1, blocking collectives, per_device(): terms = lax.all_to_all(terms, PLANE, 0, 0, tiled=True)  32.5 us
    ppermute x15, starting transfers between devices, other_core(): return lax.ppermute(block, 'core', [(0, 1), (1, 0)])  21.5 us
    all_to_all x1, starting transfers between devices, per_device(): lax.all_to_all(jnp.broadcast_to(pair, (chips, 2 * frames)), CHIPS, 0, 0,...  13 us
    unnamed x38, local copies, waits for them, and re-layouts  13 us
    ppermute x10, starting transfers between devices, ring_shift(): lax.ppermute(block, axes, [((i + offset) % size, i) for i in range(size)])  12.1 us
    pallas_call x1, Pallas kernels, per_device(): pl.pallas_call(functools.partial(delta_kernel, horizons, windows), out_sh...  8.82 us
    ppermute x10, waiting for transfers between devices, ring_shift(): lax.ppermute(block, axes, [((i + offset) % size, i) for i in range(size)])  6.3 us
    pallas_call x1, Pallas kernels, per_device(): pl.pallas_call(pred_kernel, out_shape=(jax.ShapeDtypeStruct((3, horizons...  3.42 us
  transfers between devices with their start and end apart: 27, of which 6 were waited for; matrix products, arithmetic and copies ran while one was open for 6% of the time, Pallas kernels for 9%

commit v1 on v0

--- a/solution.py
+++ b/solution.py
@@ -340,7 +340,7 @@
     smem = pl.BlockSpec(memory_space=pltpu.SMEM)
     vmem = pl.BlockSpec(memory_space=pltpu.VMEM)
     anywhere = pl.BlockSpec(memory_space=pl.ANY)
-    limit = pltpu.CompilerParams(vmem_limit_bytes=16 * 2**20)
+    limit = pltpu.CompilerParams(vmem_limit_bytes=10 * 2**20)
 
     preds, done = pl.pallas_call(
         pred_kernel,
@@ -377,7 +377,7 @@
             pltpu.VMEM((ring, 2, frames, lanes), BF16),
             pltpu.SemaphoreType.DMA((13,)),
         ],
-        compiler_params=pltpu.CompilerParams(vmem_limit_bytes=20 * 2**20),
+        compiler_params=pltpu.CompilerParams(vmem_limit_bytes=16 * 2**20),
         cost_estimate=pl.CostEstimate(
             flops=4000000000, bytes_accessed=12000000, transcendentals=900000
         ),

time: 140 us -> 140 us (level)
  no operation moved by 1% of the time
where the time goes in v1:
time: 140 us
  starting transfers between devices  46.7 us (33%)
  blocking collectives  32.5 us (23%)
  Pallas kernels  17.6 us (13%)
  between operations  15 us (11%)
  local copies, waits for them, and re-layouts  13.7 us (10%)
  waiting for transfers between devices  10.6 us (8%)
  other arithmetic  2.15 us (2%)
    all_to_all x1, blocking collectives, per_device(): terms = lax.all_to_all(terms, PLANE, 0, 0, tiled=True)  32.5 us
    ppermute x15, starting transfers between devices, other_core(): return lax.ppermute(block, 'core', [(0, 1), (1, 0)])  21.5 us
    all_to_all x1, starting transfers between devices, per_device(): lax.all_to_all(jnp.broadcast_to(pair, (chips, 2 * frames)), CHIPS, 0, 0,...  13 us
    unnamed x38, local copies, waits for them, and re-layouts  13 us
    ppermute x10, starting transfers between devices, ring_shift(): lax.ppermute(block, axes, [((i + offset) % size, i) for i in range(size)])  12.1 us
    pallas_call x1, Pallas kernels, per_device(): pl.pallas_call(functools.partial(delta_kernel, horizons, windows), out_sh...  8.82 us
    ppermute x10, waiting for transfers between devices, ring_shift(): lax.ppermute(block, axes, [((i + offset) % size, i) for i in range(size)])  6.3 us
    pallas_call x1, Pallas kernels, per_device(): pl.pallas_call(pred_kernel, out_shape=(jax.ShapeDtypeStruct((3, horizons...  3.42 us
  transfers between devices with their start and end apart: 27, of which 6 were waited for; matrix products, arithmetic and copies ran while one was open for 6% of the time, Pallas kernels for 9%

profile of v1, /device:TPU:1, one launch (start us, length us, event | category | flops | bytes accessed | tf_op | source)
XLA Modules:
  0.0 139.6 jit_solution(6768142689438076927)
XLA Ops:
  7.2 2.0 %pad_maximum_fusion.1 = bf16[128,2048]{1,0:T(8,128)(2,1)} fusion(bf16[128,1024]{1,0:T(8,128)(2,1)} %bitcast.23, bf16[128,1024]{1,0:T(8,128)(2,1)} %bitcast.28), kind=kLoop, calls=%fused_computation.2 | loop fusion | flops 1048576 | bytes 1048576 | tf_op jit(solution)/shard_map/concatenate | solution.py:338
  9.3 1.4 %convolution_convert_fusion = bf16[128,1024]{1,0:T(8,128)(2,1)S(1)} fusion(bf16[1024,1024]{1,0:T(8,128)(2,1)S(1)} %copy-done, bf16[1,128,1024]{2,1,0:T(8,128)(2,1)} %param.6), kind=kOutput, calls=%fused_computation | convolution fusion | flops 268566528 | bytes 2621440 | tf_op jit(solution)/shard_map/dot_general | solution.py:318
  10.8 3.3 %collective-permute-start.3 = (bf16[256,1024]{1,0:T(8,128)(2,1)S(1)}, bf16[256,1024]{1,0:T(8,128)(2,1)S(1)}, u32[]{:S(2)}, u32[]{:S(2)}) collective-permute-start(bf16[256,1024]{1,0:T(8,128)(2,1)S(1)} %pad_maximum_fusion.both), channel_id=1, source_target_pairs={{0,1},{1,0},{2,3},{3,2},{4,5},{5,4},{6,7},{7,6},{8,9},{9,8},{10,11... | collective-permute-start | bytes 1572872 | tf_op jit(solution)/shard_map/ppermute | solution.py:38
  14.8 0.1 collective-permute-start.2
  14.9 0.1 collective-permute-start
  15.0 4.8 %collective-permute-start.1 = (bf16[256,1024]{1,0:T(8,128)(2,1)S(1)}, bf16[256,1024]{1,0:T(8,128)(2,1)}, u32[]{:S(2)}, u32[]{:S(2)}) collective-permute-start(bf16[256,1024]{1,0:T(8,128)(2,1)S(1)} %pad_maximum_fusion.both), channel_id=1, source_target_pairs={{2,0},{3,1},{4,2},{5,3},{6,4},{7,5},{8,6},{9,7},{10,8},{11,9},{12,... | collective-permute-start | bytes 1572872 | tf_op jit(solution)/shard_map/ppermute | solution.py:30
  19.9 0.7 broadcast_in_dim.2
  20.6 13.0 %all-to-all-start = ((f32[128,1,256]{2,1,0:T(1,128)}), f32[128,1,256]{2,1,0:T(1,128)}, u32[]{:S(2)}, u32[]{:S(2)}) async-start(f32[128,1,256]{2,1,0:T(1,128)} %broadcast_in_dim.2), calls=%async_computation | async-start | bytes 262144 | tf_op jit(solution)/shard_map/all_to_all | solution.py:330
  33.6 0.6 collective-permute-start.4
  34.2 2.2 %collective-permute-start.5 = (bf16[128,1024]{1,0:T(8,128)(2,1)}, bf16[128,1024]{1,0:T(8,128)(2,1)}, u32[]{:S(2)}, u32[]{:S(2)}) collective-permute-start(bf16[128,1024]{1,0:T(8,128)(2,1)} %copy-done.9), channel_id=1, source_target_pairs={{4,0},{5,1},{6,2},{7,3},{8,4},{9,5},{10,6},{11,7},{12,8},{13,9},{1... | collective-permute-start | bytes 786440 | tf_op jit(solution)/shard_map/ppermute | solution.py:30
  36.4 5.6 %copy.10 = bf16[128,8,2,1024]{3,1,2,0:T(8,128)(2,1)} copy(bf16[128,8,2,1024]{3,2,1,0:T(2,128)(2,1)} %bitcast.27) | data formatting | bytes 8388608
  42.0 2.4 %all-to-all-done = f32[128,1,256]{2,1,0:T(1,128)} async-done(((f32[128,1,256]{2,1,0:T(1,128)}), f32[128,1,256]{2,1,0:T(1,128)}, u32[]{:S(2)}, u32[]{:S(2)}) %all-to-all-start) | async-done | bytes 131104 | tf_op jit(solution)/shard_map/all_to_all | solution.py:330
  44.3 0.9 copy.12
  45.3 3.2 %collective-permute-start.6 = (bf16[256,1024]{1,0:T(8,128)(2,1)}, bf16[256,1024]{1,0:T(8,128)(2,1)}, u32[]{:S(2)}, u32[]{:S(2)}) collective-permute-start(bf16[256,1024]{1,0:T(8,128)(2,1)} %collective-permute-done.low2), channel_id=1, source_target_pairs={{0,1},{1,0},{2,3},{3,2},{4,5},{5,4},{6,7},{7,6},{8,9},{9,8},{10,11... | collective-permute-start | bytes 1572872 | tf_op jit(solution)/shard_map/ppermute | solution.py:38
  48.5 0.1 collective-permute-start.7
  48.6 0.4 collective-permute-start.8
  49.0 0.3 collective-permute-start.9
  49.4 2.2 %copy-done.1 = bf16[128,8,2,1024]{3,1,2,0:T(8,128)(2,1)S(1)} copy-done((bf16[128,8,2,1024]{3,1,2,0:T(8,128)(2,1)S(1)}, bf16[128,8,2,1024]{3,1,2,0:T(8,128)(2,1)}, u32[]{:S(2)}) %copy-start.1) | copy-done | bytes 4194328
  51.6 3.4 %shard_map.85 = (bf16[3,256,1024]{2,1,0:T(8,128)(2,1)S(1)}, f32[1,128]{1,0:T(1,128)}) custom-call(bf16[256,1024]{1,0:T(8,128)(2,1)} %collective-permute-done.low2, bf16[128,1024]{1,0:T(8,128)(2,1)S(1)} %bitcast.25, bf16[256,1024]{1,0:T(8,128)(2,1)} %collective-permute-done.1.high2, bf16[1024,2048]{1,0:T(8,128)(2,1)S(1)} %bitcast.21), custom_call_target="tpu_custom_call" | custom-call | flops 1600000000 | bytes 6500000 | tf_op jit(solution)/shard_map/pallas_call | solution.py:345
  55.0 8.8 %shard_map.86 = (bf16[2,128,384]{2,1,0:T(8,128)(2,1)S(1)}, bf16[2,128,384]{2,1,0:T(8,128)(2,1)S(1)}, bf16[2,128,384]{2,1,0:T(8,128)(2,1)S(1)}, bf16[2,128,384]{2,1,0:T(8,128)(2,1)S(1)}, f32[1,128]{1,0:T(1,128)S(1)}) custom-call(s32[1,4]{1,0:T(1,128)S(1)} %add_bitcast_fusion.core_ref, f32[128,256]{1,0:T(8,128)S(1)} %bitcast.26, ...), custom_call_target="tpu_custom_call" | custom-call | flops 4000000000 | bytes 12000000 | tf_op jit(solution)/shard_map/pallas_call | solution.py:366
  63.9 0.7 copy-done.6
  64.5 0.7 copy-done.7
  65.2 0.7 copy-done.8
  65.9 0.2 collective-permute-start.17
  66.2 0.7 collective-permute-start.10
  66.8 1.5 %collective-permute-start.11 = (bf16[2,128,384]{2,1,0:T(8,128)(2,1)}, bf16[2,128,384]{2,1,0:T(8,128)(2,1)S(1)}, u32[]{:S(2)}, u32[]{:S(2)}) collective-permute-start(bf16[2,128,384]{2,1,0:T(8,128)(2,1)} %copy-done.7), channel_id=1, source_target_pairs={{128,0},{192,64},{0,128},{64,192},{129,1},{193,65},{1,129},{65,193... | collective-permute-start | bytes 589832 | tf_op jit(solution)/shard_map/ppermute | solution.py:30
  68.3 0.8 collective-permute-start.13
  69.1 3.5 %collective-permute-done.10.same_1 = bf16[2,128,384]{2,1,0:T(8,128)(2,1)S(1)} collective-permute-done((bf16[2,128,384]{2,1,0:T(8,128)(2,1)}, bf16[2,128,384]{2,1,0:T(8,128)(2,1)S(1)}, u32[]{:S(2)}, u32[]{:S(2)}) %collective-permute-start.10) | collective-permute-done | bytes 196640 | tf_op jit(solution)/shard_map/ppermute | solution.py:30
  72.6 1.8 %collective-permute-start.14 = (bf16[2,128,384]{2,1,0:T(8,128)(2,1)S(1)}, bf16[2,128,384]{2,1,0:T(8,128)(2,1)S(1)}, u32[]{:S(2)}, u32[]{:S(2)}) collective-permute-start(bf16[2,128,384]{2,1,0:T(8,128)(2,1)S(1)} %collective-permute-done.10.same_1), channel_id=1, source_target_pairs={{0,1},{1,0},{2,3},{3,2},{4,5},{5,4},{6,7},{7,6},{8,9},{9,8},{10,11... | collective-permute-start | bytes 589832 | tf_op jit(solution)/shard_map/ppermute | solution.py:38
  74.4 0.1 collective-permute-done.11.same_2
  74.5 2.4 %collective-permute-start.15 = (bf16[2,128,384]{2,1,0:T(8,128)(2,1)S(1)}, bf16[2,128,384]{2,1,0:T(8,128)(2,1)S(1)}, u32[]{:S(2)}, u32[]{:S(2)}) collective-permute-start(bf16[2,128,384]{2,1,0:T(8,128)(2,1)S(1)} %collective-permute-done.11.same_2), channel_id=1, source_target_pairs={{0,1},{1,0},{2,3},{3,2},{4,5},{5,4},{6,7},{7,6},{8,9},{9,8},{10,11... | collective-permute-start | bytes 589832 | tf_op jit(solution)/shard_map/ppermute | solution.py:38
  76.9 2.7 %collective-permute-done.12.same_3 = bf16[2,128,384]{2,1,0:T(8,128)(2,1)S(1)} collective-permute-done((bf16[2,128,384]{2,1,0:T(8,128)(2,1)}, bf16[2,128,384]{2,1,0:T(8,128)(2,1)S(1)}, u32[]{:S(2)}, u32[]{:S(2)}) %collective-permute-start.12) | collective-permute-done | bytes 196640 | tf_op jit(solution)/shard_map/ppermute | solution.py:30
  79.6 0.5 collective-permute-start.16
  80.1 1.1 collective-permute-done.16.cross_3
  81.2 1.6 %copy-done.3 = bf16[512,2048]{1,0:T(8,128)(2,1)S(1)} copy-done((bf16[512,2048]{1,0:T(8,128)(2,1)S(1)}, bf16[512,2048]{1,0:T(8,128)(2,1)}, u32[]{:S(2)}) %copy-start.3) | copy-done | bytes 2097176
  82.8 1.9 %shard_map.87 = bf16[32,112,128]{2,1,0:T(8,128)(2,1)S(1)} custom-call(s32[1,4]{1,0:T(1,128)S(1)} %add_bitcast_fusion.core_ref, f32[1,128]{1,0:T(1,128)S(1)} %get-tuple-element.30.loss_ref, bf16[2,128,384]{2,1,0:T(8,128)(2,1)S(1)} %get-tuple-element.31.same_0, bf16[2,128,384]{2,1,0:T(8,128)(2,1)S(1)} %collective-permute-done.10.same_1, ...), custom_call_target="tpu_custom_call" | custom-call | flops 1600000000 | bytes 6000000 | tf_op jit(solution)/shard_map/pallas_call | solution.py:393
  84.6 32.5 %all_to_all.14.terms_ref = bf16[32,112,128]{2,1,0:T(8,128)(2,1)} all-to-all(bf16[32,112,128]{2,1,0:T(8,128)(2,1)S(1)} %shard_map.87), channel_id=1, replica_groups=mesh['y'=4,'xh'=2,'z'=8,'xl'=2,'core'=2] {'xh','z','xl'}, dimensions={0} | all-to-all | bytes 1835008 | tf_op jit(solution)/shard_map/all_to_all | solution.py:404
  117.1 2.0 %shard_map.88 = (f32[2,8,384]{2,1,0:T(8,128)}, f32[2,8,384]{2,1,0:T(8,128)}, f32[2,8,384]{2,1,0:T(8,128)}, f32[2,8,384]{2,1,0:T(8,128)}) custom-call(s32[1,4]{1,0:T(1,128)} %copy-done.5, bf16[32,112,128]{2,1,0:T(8,128)(2,1)} %all_to_all.14.terms_ref), custom_call_target="tpu_custom_call" | custom-call | tf_op jit(solution)/shard_map/pallas_call | solution.py:406
  119.1 0.7 collective-permute-start.18
  119.8 1.0 collective-permute-start.19
  120.8 0.5 collective-permute-start.20
  121.4 4.0 %collective-permute-start.21 = (f32[2,8,384]{2,1,0:T(8,128)}, f32[2,8,384]{2,1,0:T(8,128)S(1)}, u32[]{:S(2)}, u32[]{:S(2)}) collective-permute-start(f32[2,8,384]{2,1,0:T(8,128)} %get-tuple-element.36.same_0), channel_id=1, source_target_pairs={{0,1},{1,0},{2,3},{3,2},{4,5},{5,4},{6,7},{7,6},{8,9},{9,8},{10,11... | collective-permute-start | bytes 73736 | tf_op jit(solution)/shard_map/ppermute | solution.py:38
  125.3 0.9 collective-permute-start.22
  126.2 2.3 %collective-permute-start.23 = (f32[2,8,384]{2,1,0:T(8,128)S(1)}, f32[2,8,384]{2,1,0:T(8,128)S(1)}, u32[]{:S(2)}, u32[]{:S(2)}) collective-permute-start(f32[2,8,384]{2,1,0:T(8,128)S(1)} %collective-permute-done.19.same_2), channel_id=1, source_target_pairs={{0,1},{1,0},{2,3},{3,2},{4,5},{5,4},{6,7},{7,6},{8,9},{9,8},{10,11... | collective-permute-start | bytes 73736 | tf_op jit(solution)/shard_map/ppermute | solution.py:38
  128.5 1.2 collective-permute-start.24
  129.8 0.8 collective-permute-done.24.cross_3
  130.6 0.6 copy-done.16
  131.2 1.5 %shard_map.89 = (f32[1,1]{1,0:T(1,128)}, f32[4,2,1024]{2,1,0:T(2,128)}, f32[4,1024]{1,0:T(4,128)}) custom-call(s32[1,4]{1,0:T(1,128)} %copy-done.5, f32[2,8,384]{2,1,0:T(8,128)} %get-tuple-element.36.same_0, f32[2,8,384]{2,1,0:T(8,128)} %copy-done.10, f32[2,8,384]{2,1,0:T(8,128)} %copy-done.11, f32[2,8,384]{2,1,0:T(8,128)} %copy-done.12, ...), custom_call_target="tpu_custom_call" | custom-call | tf_op jit(solution)/shard_map/pallas_call | solution.py:415
  (59 shorter events, 0.3 us)
Async XLA Ops:
  7.2 2.1 %copy-start = (bf16[1024,1024]{1,0:T(8,128)(2,1)S(1)}, bf16[1024,1024]{1,0:T(8,128)(2,1)}, u32[]{:S(2)}) copy-start(bf16[1024,1024]{1,0:T(8,128)(2,1)} %param.9) | copy-start | bytes 6291460
  7.2 58.7 %all-gather.2.cloned.1.call-start = ((), (), s32[]{:S(2)}) async-start(), calls=%async_computation.2 | async-start | bytes 2621440 | tf_op jit(solution)/shard_map/all_gather | solution.py:338
  7.2 3.5 %copy-start.4 = (bf16[1,128,1024]{2,1,0:T(8,128)(2,1)S(1)}, bf16[1,128,1024]{2,1,0:T(8,128)(2,1)}, u32[]{:S(2)}) copy-start(bf16[1,128,1024]{2,1,0:T(8,128)(2,1)} %param.7) | copy-start | bytes 786436
  9.3 5.5 %copy-start.17 = (s32[1,128]{1,0:T(1,128)S(1)}, s32[1,128]{1,0:T(1,128)}, u32[]{:S(2)}) copy-start(s32[1,128]{1,0:T(1,128)} %param.11) | copy-start | bytes 1540
  10.7 4.2 %copy-start.9 = (bf16[128,1024]{1,0:T(8,128)(2,1)}, bf16[128,1024]{1,0:T(8,128)(2,1)S(1)}, u32[]{:S(2)}) copy-start(bf16[128,1024]{1,0:T(8,128)(2,1)S(1)} %convolution_convert_fusion) | copy-start | bytes 786436
  10.8 9.1 %collective-permute-start.3 = (bf16[256,1024]{1,0:T(8,128)(2,1)S(1)}, bf16[256,1024]{1,0:T(8,128)(2,1)S(1)}, u32[]{:S(2)}, u32[]{:S(2)}) collective-permute-start(bf16[256,1024]{1,0:T(8,128)(2,1)S(1)} %pad_maximum_fusion.both), channel_id=1, source_target_pairs={{0,1},{1,0},{2,3},{3,2},{4,5},{5,4},{6,7},{7,6},{8,9},{9,8},{10,11... | collective-permute-start | bytes 1572872 | tf_op jit(solution)/shard_map/ppermute | solution.py:38
  14.8 5.1 %collective-permute-start.2 = (f32[1,128]{1,0:T(1,128)S(1)}, f32[1,128]{1,0:T(1,128)S(1)}, u32[]{:S(2)}, u32[]{:S(2)}) collective-permute-start(f32[1,128]{1,0:T(1,128)S(1)} %and_convert_fusion), channel_id=1, source_target_pairs={{0,1},{1,0},{2,3},{3,2},{4,5},{5,4},{6,7},{7,6},{8,9},{9,8},{10,11... | collective-permute-start | bytes 1544 | tf_op jit(solution)/shard_map/ppermute | solution.py:38
  14.9 30.4 %collective-permute-start = (bf16[256,1024]{1,0:T(8,128)(2,1)S(1)}, bf16[256,1024]{1,0:T(8,128)(2,1)}, u32[]{:S(2)}, u32[]{:S(2)}) collective-permute-start(bf16[256,1024]{1,0:T(8,128)(2,1)S(1)} %pad_maximum_fusion.both), channel_id=1, source_target_pairs={{30,0},{31,1},{0,2},{1,3},{2,4},{3,5},{4,6},{5,7},{6,8},{7,9},{8,1... | collective-permute-start | bytes 1572872 | tf_op jit(solution)/shard_map/ppermute | solution.py:30
  15.0 30.3 %collective-permute-start.1 = (bf16[256,1024]{1,0:T(8,128)(2,1)S(1)}, bf16[256,1024]{1,0:T(8,128)(2,1)}, u32[]{:S(2)}, u32[]{:S(2)}) collective-permute-start(bf16[256,1024]{1,0:T(8,128)(2,1)S(1)} %pad_maximum_fusion.both), channel_id=1, source_target_pairs={{2,0},{3,1},{4,2},{5,3},{6,4},{7,5},{8,6},{9,7},{10,8},{11,9},{12,... | collective-permute-start | bytes 1572872 | tf_op jit(solution)/shard_map/ppermute | solution.py:30
  20.6 23.8 %all-to-all-start = ((f32[128,1,256]{2,1,0:T(1,128)}), f32[128,1,256]{2,1,0:T(1,128)}, u32[]{:S(2)}, u32[]{:S(2)}) async-start(f32[128,1,256]{2,1,0:T(1,128)} %broadcast_in_dim.2), calls=%async_computation | async-start | bytes 262144 | tf_op jit(solution)/shard_map/all_to_all | solution.py:330
  33.6 15.0 %collective-permute-start.4 = (bf16[128,1024]{1,0:T(8,128)(2,1)}, bf16[128,1024]{1,0:T(8,128)(2,1)}, u32[]{:S(2)}, u32[]{:S(2)}) collective-permute-start(bf16[128,1024]{1,0:T(8,128)(2,1)} %copy-done.9), channel_id=1, source_target_pairs={{28,0},{29,1},{30,2},{31,3},{0,4},{1,5},{2,6},{3,7},{4,8},{5,9},{6... | collective-permute-start | bytes 786440 | tf_op jit(solution)/shard_map/ppermute | solution.py:30
  34.2 14.8 %collective-permute-start.5 = (bf16[128,1024]{1,0:T(8,128)(2,1)}, bf16[128,1024]{1,0:T(8,128)(2,1)}, u32[]{:S(2)}, u32[]{:S(2)}) collective-permute-start(bf16[128,1024]{1,0:T(8,128)(2,1)} %copy-done.9), channel_id=1, source_target_pairs={{4,0},{5,1},{6,2},{7,3},{8,4},{9,5},{10,6},{11,7},{12,8},{13,9},{1... | collective-permute-start | bytes 786440 | tf_op jit(solution)/shard_map/ppermute | solution.py:30
  45.3 9.7 %collective-permute-start.6 = (bf16[256,1024]{1,0:T(8,128)(2,1)}, bf16[256,1024]{1,0:T(8,128)(2,1)}, u32[]{:S(2)}, u32[]{:S(2)}) collective-permute-start(bf16[256,1024]{1,0:T(8,128)(2,1)} %collective-permute-done.low2), channel_id=1, source_target_pairs={{0,1},{1,0},{2,3},{3,2},{4,5},{5,4},{6,7},{7,6},{8,9},{9,8},{10,11... | collective-permute-start | bytes 1572872 | tf_op jit(solution)/shard_map/ppermute | solution.py:38
  48.5 6.5 %collective-permute-start.7 = (bf16[256,1024]{1,0:T(8,128)(2,1)}, bf16[256,1024]{1,0:T(8,128)(2,1)}, u32[]{:S(2)}, u32[]{:S(2)}) collective-permute-start(bf16[256,1024]{1,0:T(8,128)(2,1)} %collective-permute-done.1.high2), channel_id=1, source_target_pairs={{0,1},{1,0},{2,3},{3,2},{4,5},{5,4},{6,7},{7,6},{8,9},{9,8},{10,11... | collective-permute-start | bytes 1572872 | tf_op jit(solution)/shard_map/ppermute | solution.py:38
  48.6 6.4 %collective-permute-start.8 = (bf16[128,1024]{1,0:T(8,128)(2,1)}, bf16[128,1024]{1,0:T(8,128)(2,1)S(1)}, u32[]{:S(2)}, u32[]{:S(2)}) collective-permute-start(bf16[128,1024]{1,0:T(8,128)(2,1)} %collective-permute-done.4.low4), channel_id=1, source_target_pairs={{0,1},{1,0},{2,3},{3,2},{4,5},{5,4},{6,7},{7,6},{8,9},{9,8},{10,11... | collective-permute-start | bytes 786440 | tf_op jit(solution)/shard_map/ppermute | solution.py:38
  49.0 6.0 %collective-permute-start.9 = (bf16[128,1024]{1,0:T(8,128)(2,1)}, bf16[128,1024]{1,0:T(8,128)(2,1)S(1)}, u32[]{:S(2)}, u32[]{:S(2)}) collective-permute-start(bf16[128,1024]{1,0:T(8,128)(2,1)} %collective-permute-done.5.high4), channel_id=1, source_target_pairs={{0,1},{1,0},{2,3},{3,2},{4,5},{5,4},{6,7},{7,6},{8,9},{9,8},{10,11... | collective-permute-start | bytes 786440 | tf_op jit(solution)/shard_map/ppermute | solution.py:38
  49.4 2.2 %copy-start.1 = (bf16[128,8,2,1024]{3,1,2,0:T(8,128)(2,1)S(1)}, bf16[128,8,2,1024]{3,1,2,0:T(8,128)(2,1)}, u32[]{:S(2)}) copy-start(bf16[128,8,2,1024]{3,1,2,0:T(8,128)(2,1)} %copy.10) | copy-start | bytes 12582916
  51.6 29.6 %copy-start.5 = (s32[1,4]{1,0:T(1,128)}, s32[1,4]{1,0:T(1,128)S(1)}, u32[]{:S(2)}) copy-start(s32[1,4]{1,0:T(1,128)S(1)} %add_bitcast_fusion.core_ref) | copy-start | bytes 52
  51.6 3.5 %copy-start.2 = (bf16[128,8,2,1024]{3,1,2,0:T(8,128)(2,1)S(1)}, bf16[128,8,2,1024]{3,1,2,0:T(8,128)(2,1)}, u32[]{:S(2)}) copy-start(bf16[128,8,2,1024]{3,1,2,0:T(8,128)(2,1)} %copy.10) | copy-start | bytes 12582916
  63.9 0.7 copy-start.6
  64.5 0.7 copy-start.7
  65.2 0.7 copy-start.8
  65.9 15.2 %collective-permute-start.17 = (bf16[512,2048]{1,0:T(8,128)(2,1)}, bf16[512,2048]{1,0:T(8,128)(2,1)S(1)}, u32[]{:S(2)}, u32[]{:S(2)}) collective-permute-start(bf16[512,2048]{1,0:T(8,128)(2,1)} %all-gather.2.cloned.1.call-done.rows_same), channel_id=1, source_target_pairs={{0,1},{1,0},{2,3},{3,2},{4,5},{5,4},{6,7},{7,6},{8,9},{9,8},{10,11... | collective-permute-start | bytes 6291464 | tf_op jit(solution)/shard_map/ppermute | solution.py:38
  66.2 6.4 %collective-permute-start.10 = (bf16[2,128,384]{2,1,0:T(8,128)(2,1)}, bf16[2,128,384]{2,1,0:T(8,128)(2,1)S(1)}, u32[]{:S(2)}, u32[]{:S(2)}) collective-permute-start(bf16[2,128,384]{2,1,0:T(8,128)(2,1)} %copy-done.8), channel_id=1, source_target_pairs={{64,0},{128,64},{192,128},{0,192},{65,1},{129,65},{193,129},{1,193... | collective-permute-start | bytes 589832 | tf_op jit(solution)/shard_map/ppermute | solution.py:30
  66.8 7.7 %collective-permute-start.11 = (bf16[2,128,384]{2,1,0:T(8,128)(2,1)}, bf16[2,128,384]{2,1,0:T(8,128)(2,1)S(1)}, u32[]{:S(2)}, u32[]{:S(2)}) collective-permute-start(bf16[2,128,384]{2,1,0:T(8,128)(2,1)} %copy-done.7), channel_id=1, source_target_pairs={{128,0},{192,64},{0,128},{64,192},{129,1},{193,65},{1,129},{65,193... | collective-permute-start | bytes 589832 | tf_op jit(solution)/shard_map/ppermute | solution.py:30
  68.3 11.3 %collective-permute-start.12 = (bf16[2,128,384]{2,1,0:T(8,128)(2,1)}, bf16[2,128,384]{2,1,0:T(8,128)(2,1)S(1)}, u32[]{:S(2)}, u32[]{:S(2)}) collective-permute-start(bf16[2,128,384]{2,1,0:T(8,128)(2,1)} %copy-done.6), channel_id=1, source_target_pairs={{192,0},{0,64},{64,128},{128,192},{193,1},{1,65},{65,129},{129,193... | collective-permute-start | bytes 589832 | tf_op jit(solution)/shard_map/ppermute | solution.py:30
  68.3 11.8 %collective-permute-start.13 = (bf16[2,128,384]{2,1,0:T(8,128)(2,1)S(1)}, bf16[2,128,384]{2,1,0:T(8,128)(2,1)S(1)}, u32[]{:S(2)}, u32[]{:S(2)}) collective-permute-start(bf16[2,128,384]{2,1,0:T(8,128)(2,1)S(1)} %get-tuple-element.31.same_0), channel_id=1, source_target_pairs={{0,1},{1,0},{2,3},{3,2},{4,5},{5,4},{6,7},{7,6},{8,9},{9,8},{10,11... | collective-permute-start | bytes 589832 | tf_op jit(solution)/shard_map/ppermute | solution.py:38
  72.6 7.5 %collective-permute-start.14 = (bf16[2,128,384]{2,1,0:T(8,128)(2,1)S(1)}, bf16[2,128,384]{2,1,0:T(8,128)(2,1)S(1)}, u32[]{:S(2)}, u32[]{:S(2)}) collective-permute-start(bf16[2,128,384]{2,1,0:T(8,128)(2,1)S(1)} %collective-permute-done.10.same_1), channel_id=1, source_target_pairs={{0,1},{1,0},{2,3},{3,2},{4,5},{5,4},{6,7},{7,6},{8,9},{9,8},{10,11... | collective-permute-start | bytes 589832 | tf_op jit(solution)/shard_map/ppermute | solution.py:38
  74.5 5.6 %collective-permute-start.15 = (bf16[2,128,384]{2,1,0:T(8,128)(2,1)S(1)}, bf16[2,128,384]{2,1,0:T(8,128)(2,1)S(1)}, u32[]{:S(2)}, u32[]{:S(2)}) collective-permute-start(bf16[2,128,384]{2,1,0:T(8,128)(2,1)S(1)} %collective-permute-done.11.same_2), channel_id=1, source_target_pairs={{0,1},{1,0},{2,3},{3,2},{4,5},{5,4},{6,7},{7,6},{8,9},{9,8},{10,11... | collective-permute-start | bytes 589832 | tf_op jit(solution)/shard_map/ppermute | solution.py:38
  79.6 1.6 %collective-permute-start.16 = (bf16[2,128,384]{2,1,0:T(8,128)(2,1)S(1)}, bf16[2,128,384]{2,1,0:T(8,128)(2,1)S(1)}, u32[]{:S(2)}, u32[]{:S(2)}) collective-permute-start(bf16[2,128,384]{2,1,0:T(8,128)(2,1)S(1)} %collective-permute-done.12.same_3), channel_id=1, source_target_pairs={{0,1},{1,0},{2,3},{3,2},{4,5},{5,4},{6,7},{7,6},{8,9},{9,8},{10,11... | collective-permute-start | bytes 589832 | tf_op jit(solution)/shard_map/ppermute | solution.py:38
  81.2 1.6 %copy-start.3 = (bf16[512,2048]{1,0:T(8,128)(2,1)S(1)}, bf16[512,2048]{1,0:T(8,128)(2,1)}, u32[]{:S(2)}) copy-start(bf16[512,2048]{1,0:T(8,128)(2,1)} %all-gather.2.cloned.1.call-done.rows_same) | copy-start | bytes 6291460
  119.1 6.2 %collective-permute-start.18 = (f32[2,8,384]{2,1,0:T(8,128)}, f32[2,8,384]{2,1,0:T(8,128)S(1)}, u32[]{:S(2)}, u32[]{:S(2)}) collective-permute-start(f32[2,8,384]{2,1,0:T(8,128)} %get-tuple-element.37), channel_id=1, source_target_pairs={{64,0},{128,64},{192,128},{0,192},{65,1},{129,65},{193,129},{1,193... | collective-permute-start | bytes 73736 | tf_op jit(solution)/shard_map/ppermute | solution.py:30
  119.8 6.5 %collective-permute-start.19 = (f32[2,8,384]{2,1,0:T(8,128)}, f32[2,8,384]{2,1,0:T(8,128)S(1)}, u32[]{:S(2)}, u32[]{:S(2)}) collective-permute-start(f32[2,8,384]{2,1,0:T(8,128)} %get-tuple-element.38), channel_id=1, source_target_pairs={{128,0},{192,64},{0,128},{64,192},{129,1},{193,65},{1,129},{65,193... | collective-permute-start | bytes 73736 | tf_op jit(solution)/shard_map/ppermute | solution.py:30
  120.8 7.7 %collective-permute-start.20 = (f32[2,8,384]{2,1,0:T(8,128)}, f32[2,8,384]{2,1,0:T(8,128)S(1)}, u32[]{:S(2)}, u32[]{:S(2)}) collective-permute-start(f32[2,8,384]{2,1,0:T(8,128)} %get-tuple-element.39), channel_id=1, source_target_pairs={{192,0},{0,64},{64,128},{128,192},{193,1},{1,65},{65,129},{129,193... | collective-permute-start | bytes 73736 | tf_op jit(solution)/shard_map/ppermute | solution.py:30
  121.4 8.4 %collective-permute-start.21 = (f32[2,8,384]{2,1,0:T(8,128)}, f32[2,8,384]{2,1,0:T(8,128)S(1)}, u32[]{:S(2)}, u32[]{:S(2)}) collective-permute-start(f32[2,8,384]{2,1,0:T(8,128)} %get-tuple-element.36.same_0), channel_id=1, source_target_pairs={{0,1},{1,0},{2,3},{3,2},{4,5},{5,4},{6,7},{7,6},{8,9},{9,8},{10,11... | collective-permute-start | bytes 73736 | tf_op jit(solution)/shard_map/ppermute | solution.py:38
  125.3 5.3 %copy-start.10 = (f32[2,8,384]{2,1,0:T(8,128)}, f32[2,8,384]{2,1,0:T(8,128)S(1)}, u32[]{:S(2)}) copy-start(f32[2,8,384]{2,1,0:T(8,128)S(1)} %collective-permute-done.18.same_1) | copy-start | bytes 73732
  125.3 4.4 %collective-permute-start.22 = (f32[2,8,384]{2,1,0:T(8,128)S(1)}, f32[2,8,384]{2,1,0:T(8,128)S(1)}, u32[]{:S(2)}, u32[]{:S(2)}) collective-permute-start(f32[2,8,384]{2,1,0:T(8,128)S(1)} %collective-permute-done.18.same_1), channel_id=1, source_target_pairs={{0,1},{1,0},{2,3},{3,2},{4,5},{5,4},{6,7},{7,6},{8,9},{9,8},{10,11... | collective-permute-start | bytes 73736 | tf_op jit(solution)/shard_map/ppermute | solution.py:38
  126.2 4.4 %copy-start.11 = (f32[2,8,384]{2,1,0:T(8,128)}, f32[2,8,384]{2,1,0:T(8,128)S(1)}, u32[]{:S(2)}) copy-start(f32[2,8,384]{2,1,0:T(8,128)S(1)} %collective-permute-done.19.same_2) | copy-start | bytes 73732
  126.2 3.5 %collective-permute-start.23 = (f32[2,8,384]{2,1,0:T(8,128)S(1)}, f32[2,8,384]{2,1,0:T(8,128)S(1)}, u32[]{:S(2)}, u32[]{:S(2)}) collective-permute-start(f32[2,8,384]{2,1,0:T(8,128)S(1)} %collective-permute-done.19.same_2), channel_id=1, source_target_pairs={{0,1},{1,0},{2,3},{3,2},{4,5},{5,4},{6,7},{7,6},{8,9},{9,8},{10,11... | collective-permute-start | bytes 73736 | tf_op jit(solution)/shard_map/ppermute | solution.py:38
  128.5 2.1 %copy-start.12 = (f32[2,8,384]{2,1,0:T(8,128)}, f32[2,8,384]{2,1,0:T(8,128)S(1)}, u32[]{:S(2)}) copy-start(f32[2,8,384]{2,1,0:T(8,128)S(1)} %collective-permute-done.20.same_3) | copy-start | bytes 73732
  128.5 2.1 %collective-permute-start.24 = (f32[2,8,384]{2,1,0:T(8,128)S(1)}, f32[2,8,384]{2,1,0:T(8,128)S(1)}, u32[]{:S(2)}, u32[]{:S(2)}) collective-permute-start(f32[2,8,384]{2,1,0:T(8,128)S(1)} %collective-permute-done.20.same_3), channel_id=1, source_target_pairs={{0,1},{1,0},{2,3},{3,2},{4,5},{5,4},{6,7},{7,6},{8,9},{9,8},{10,11... | collective-permute-start | bytes 73736 | tf_op jit(solution)/shard_map/ppermute | solution.py:38
  129.7 0.9 copy-start.13
  129.8 0.9 copy-start.14
  129.8 0.8 copy-start.15
  130.6 0.6 copy-start.16
Sparse Core Ops, SparseCore 0:
  9.8 38.6 all-gather.1
